TPU v7x, 256 devices: a whole 4x4x8 slice. The times are simulated.
256 devices in a mesh: curve: 128 (over z, x, y), field: 2 (over core).
Axes of the slice: x: 4, y: 4, z: 8, core: 2. Of those that a mesh axis runs over, the one named last changes fastest.
Arguments:
- atm_flux: float32 [64, 524288], P('field', 'curve'), may hold values from 0.5 to 2
- ocean_state: float32 [64, 1048576], P('field', 'curve'), may hold values from 0.5 to 2
- area_atm: float32 [524288], P('curve'), may hold values from 0.5 to 18, as said below
- area_ocean: float32 [1048576], P('curve'), may hold values from 0.5 to 18, as said below
- tiles: float32 [16384, 128, 128], P('curve'), may hold values from 0 to 0.0078125
- tile_row: int32 [16384], P('curve'), may hold values from 0 to 8191, as said below
- tile_col: int32 [16384], P('curve'), may hold values from 0 to 4095, as said below
- tile_count: int32 [128], P('curve'), may hold values from 16 to 128, as said below
Outputs:
- ocean_flux: float32 [64, 1048576], P('field', 'curve')
- atm_fixed: float32 [64, 524288], P('field', 'curve')
Inputs may be any that keep to these rules, and one draw needn't show every extreme that they name: `tile_row`: slots of device d name ocean blocks of that device, d * 64 to (d + 1) * 64 - 1. `tile_col`: slots of device d name atmosphere blocks within 16 blocks of that device's own blocks d * 32 to (d + 1) * 32 - 1, counted around the closed curve of 4096 blocks; the first slot of every device names d * 32 + 47 and the second d * 32 - 16, around the curve. `tile_count`: the live slots of a device are its first ones; the others are not part of the remap; some device has all 128 slots live. `area_atm`: positive. `area_ocean`: positive.
All inputs are finite; a program needn't handle non-finite values.
Results may differ from a plain program's by a relative error of at most 0.0003.
Values sent between devices are 32-bit elements; how exact they have to be, the bound alone decides.
A program may use at most 64 MiB of HBM per device.

v0:
```python
import jax
import jax.numpy as jnp
from jax import lax
from jax.sharding import PartitionSpec as P


def with_halo(block, sides, width):
    for axis, dim in sides:
        count = lax.axis_size(axis)
        forward = [(i, i + 1) for i in range(count - 1)]
        forward.append((count - 1, 0))
        backward = [(target, source) for source, target in forward]
        low = lax.ppermute(
            lax.slice_in_dim(block, block.shape[dim] - width, None, axis=dim), axis, forward
        )
        high = lax.ppermute(lax.slice_in_dim(block, 0, width, axis=dim), axis, backward)
        block = jnp.concatenate([low, block, high], axis=dim)
    return block


def from_behind(shard, axis, by):
    size = lax.axis_size(axis)
    return lax.ppermute(shard, axis, [(i, (i + by) % size) for i in range(size)])


def slot_terms(
    weights,
    slot_rows,
    slot_cols,
    live_slots,
    source_blocks,
    weighted_blocks,
    ocean_span,
    window_span,
):
    exact_mode = lax.Precision.HIGHEST
    forward = jnp.einsum(
        "tij,ftj->fti", weights, source_blocks[:, slot_cols, :], precision=exact_mode
    )
    row_onehot = (slot_rows[:, None] == jnp.arange(ocean_span, dtype=jnp.int32)[None, :]).astype(
        jnp.float32
    )
    row_onehot = row_onehot * live_slots[:, None]
    ocean_part = jnp.einsum("to,fti->foi", row_onehot, forward, precision=exact_mode)
    backward = jnp.einsum(
        "tij,fti->ftj", weights, weighted_blocks[:, slot_rows, :], precision=exact_mode
    )
    col_onehot = (slot_cols[:, None] == jnp.arange(window_span, dtype=jnp.int32)[None, :]).astype(
        jnp.float32
    )
    col_onehot = col_onehot * live_slots[:, None]
    window_part = jnp.einsum("tw,ftj->fwj", col_onehot, backward, precision=exact_mode)
    return (ocean_part, window_part)


def on_device(atm_flux, ocean_state, area_atm, area_ocean, tiles, tile_row, tile_col, tile_count):
    local_fields, atm_cells = atm_flux.shape
    slot_cap, block_size = (tiles.shape[0], tiles.shape[1])
    atm_span = atm_cells // block_size
    ocean_span = ocean_state.shape[1] // block_size
    margin_blocks = atm_span // 2
    window_span = atm_span + 2 * margin_blocks
    devices = lax.axis_size("curve")
    position = lax.axis_index("curve")
    extended = with_halo(atm_flux, (("curve", 1),), margin_blocks * block_size)
    source_blocks = extended.reshape(local_fields, window_span, block_size)
    weighted_blocks = (ocean_state * area_ocean[None, :]).reshape(
        local_fields, ocean_span, block_size
    )
    local_row = tile_row - position * ocean_span
    local_col = (tile_col - position * atm_span + margin_blocks) % (atm_span * devices)
    live_count = tile_count[0]
    live_slots = (jnp.arange(slot_cap, dtype=jnp.int32) < live_count).astype(jnp.float32)
    ocean_part, window_part = slot_terms(
        tiles,
        local_row,
        local_col,
        live_slots,
        source_blocks,
        weighted_blocks,
        ocean_span,
        window_span,
    )
    ocean_remap = ocean_part.reshape(local_fields, ocean_span * block_size)
    target_ocean = jnp.sum(atm_flux * area_atm[None, :], axis=1)
    got_ocean = jnp.sum(ocean_remap * area_ocean[None, :], axis=1)
    target_atm = jnp.sum(ocean_state * area_ocean[None, :], axis=1)
    target_ocean, got_ocean = lax.psum((target_ocean, got_ocean), "curve")
    window_flat = window_part.reshape(local_fields, window_span * block_size)
    rim_cells = margin_blocks * block_size
    core_cells = atm_span * block_size
    lower_part = window_flat[:, :rim_cells]
    upper_part = window_flat[:, rim_cells + core_cells :]
    core_part = window_flat[:, rim_cells : rim_cells + core_cells]
    from_below = from_behind(upper_part, "curve", 1)
    from_above = from_behind(lower_part, "curve", -1)
    back_sum = core_part + jnp.pad(from_below, ((0, 0), (0, core_cells - rim_cells)))
    back_sum = back_sum + jnp.pad(from_above, ((0, 0), (core_cells - rim_cells, 0)))
    got_atm = jnp.sum(back_sum, axis=1)
    target_atm, got_atm = lax.psum((target_atm, got_atm), "curve")
    ocean_flux = ocean_remap * (target_ocean / got_ocean)[:, None]
    atm_fixed = back_sum / area_atm[None, :] * (target_atm / got_atm)[:, None]
    return (ocean_flux, atm_fixed)


def solution(mesh):
    in_specs = (
        P("field", "curve"),
        P("field", "curve"),
        P("curve"),
        P("curve"),
        P("curve", None, None),
        P("curve"),
        P("curve"),
        P("curve"),
    )
    out_specs = (P("field", "curve"), P("field", "curve"))
    return jax.shard_map(
        on_device, mesh=mesh, in_specs=in_specs, out_specs=out_specs, check_vma=False
    )
```

profile of v0, /device:TPU:8, one launch (start us, length us, event | category | flops | bytes accessed | tf_op | source)
XLA Modules:
  0.0 405.3 jit_solution(12517144472181096281)
XLA Ops:
  0.6 1.8 fusion.31
  2.5 1.6 collective-permute-start
  4.0 0.6 collective-permute-start.1
  5.3 0.7 compare_select_fusion
  6.0 1.4 multiply_bitcast_fusion
  7.4 0.1 copy.29
  7.6 0.8 gather_fusion.1
  8.4 9.5 %fusion.11 = f32[32,128,128]{2,0,1:T(8,128)S(1)} fusion(f32[128,128,128]{2,1,0:T(8,128)} %param.12, f32[128,32,128]{2,1,0:T(8,128)S(1)} %gather_fusion.1), kind=kOutput, calls=%fused_computation.11 | convolution fusion | flops 805306368 | bytes 12582912 | tf_op jit(solution)/shard_map/tij,fti->ftj/dot_general | solution.py:45
  17.9 2.5 fusion.4
  20.4 0.0 copy-start.2
  20.5 0.0 copy-start.4
  20.5 0.6 copy.28
  21.1 0.9 fusion.30
  22.0 1.4 collective-permute-start.2
  23.4 7.4 %collective-permute-start.3 = (f32[32,2048]{1,0:T(8,128)}, f32[32,2048]{1,0:T(8,128)}, u32[]{:S(2)}, u32[]{:S(2)}) collective-permute-start(f32[32,2048]{1,0:T(8,128)} %get-tuple-element.13), channel_id=1, source_target_pairs={{0,254},{2,0},{4,2},{6,4},{8,6},{10,8},{12,10},{14,12},{16,14},{18... | collective-permute-start | bytes 786440 | tf_op jit(solution)/shard_map/ppermute | solution.py:23
  30.8 0.2 multiply_reduce_fusion.1
  31.0 1.2 copy_bitcast_fusion.2
  32.2 0.8 gather_fusion
  33.0 15.4 %fusion.8 = f32[32,128,128]{2,0,1:T(8,128)S(1)} fusion(f32[128,128,128]{2,1,0:T(8,128)} %param.12, f32[128,32,128]{2,1,0:T(8,128)S(1)} %gather_fusion), kind=kOutput, calls=%fused_computation.10 | convolution fusion | flops 805306368 | bytes 12582912 | tf_op jit(solution)/shard_map/tij,ftj->fti/dot_general | solution.py:37
  48.4 2.7 fusion.14
  51.1 1.1 fusion.16
  52.2 349.6 %all-reduce.2 = (f32[32]{0:T(128)S(1)}, f32[32]{0:T(128)S(1)}, f32[32]{0:T(128)S(1)}, f32[32]{0:T(128)S(1)}) all-reduce(f32[32]{0:T(128)S(1)} %multiply_reduce_fusion.1, f32[32]{0:T(128)S(1)} %get-tuple-element.16, f32[32]{0:T(128)S(1)} %get-tuple-element.11, f32[32]{0:T(128)S(1)} %fusion.16), channel_id=1, replica_groups=mesh['curve'=128,'field'=2] {'curve'}, use_global_device_ids=true, to_apply=%region_1.2 | all-reduce | flops 128 | bytes 1024 | tf_op jit(solution)/shard_map/psum | solution.py:88
  401.8 1.6 bitcast_multiply_fusion
  403.4 1.8 divide_multiply_fusion
  (20 shorter events, 0.1 us)
Async XLA Ops:
  2.5 28.5 %collective-permute-start = (f32[32,2048]{1,0:T(8,128)}, f32[32,2048]{1,0:T(8,128)}, u32[]{:S(2)}, u32[]{:S(2)}) collective-permute-start(f32[32,2048]{1,0:T(8,128)} %get-tuple-element.14), channel_id=1, source_target_pairs={{0,2},{2,4},{4,6},{6,8},{8,10},{10,12},{12,14},{14,16},{16,18},{18... | collective-permute-start | bytes 786440 | tf_op jit(solution)/shard_map/ppermute | solution.py:13
  4.0 26.9 %collective-permute-start.1 = (f32[32,2048]{1,0:T(8,128)}, f32[32,2048]{1,0:T(8,128)}, u32[]{:S(2)}, u32[]{:S(2)}) collective-permute-start(f32[32,2048]{1,0:T(8,128)} %get-tuple-element.15), channel_id=1, source_target_pairs={{2,0},{4,2},{6,4},{8,6},{10,8},{12,10},{14,12},{16,14},{18,16},{20... | collective-permute-start | bytes 786440 | tf_op jit(solution)/shard_map/ppermute | solution.py:16
  6.0 1.6 copy-start.5
  20.4 10.4 %copy-start.2 = (f32[32,4096]{1,0:T(8,128)S(1)}, f32[32,4096]{1,0:T(8,128)}, u32[]{:S(2)}) copy-start(f32[32,4096]{1,0:T(8,128)} %param.8) | copy-start | bytes 1572868
  20.5 10.3 %copy-start.4 = (f32[4096]{0:T(1024)S(1)}, f32[4096]{0:T(1024)}, u32[]{:S(2)}) copy-start(f32[4096]{0:T(1024)} %param.10) | copy-start | bytes 49156
  21.1 9.9 %copy-start = (f32[4,8,64,128]{3,1,2,0:T(8,128)}, f32[4,8,64,128]{3,1,2,0:T(8,128)S(1)}, u32[]{:S(2)}) copy-start(f32[4,8,64,128]{3,1,2,0:T(8,128)S(1)} %copy.28) | copy-start | bytes 3145732
  22.0 29.1 %collective-permute-start.2 = (f32[32,2048]{1,0:T(8,128)}, f32[32,2048]{1,0:T(8,128)S(1)}, u32[]{:S(2)}, u32[]{:S(2)}) collective-permute-start(f32[32,2048]{1,0:T(8,128)} %get-tuple-element.12), channel_id=1, source_target_pairs={{0,2},{2,4},{4,6},{6,8},{8,10},{10,12},{12,14},{14,16},{16,18},{18... | collective-permute-start | bytes 786440 | tf_op jit(solution)/shard_map/ppermute | solution.py:23
  23.4 27.7 %collective-permute-start.3 = (f32[32,2048]{1,0:T(8,128)}, f32[32,2048]{1,0:T(8,128)}, u32[]{:S(2)}, u32[]{:S(2)}) collective-permute-start(f32[32,2048]{1,0:T(8,128)} %get-tuple-element.13), channel_id=1, source_target_pairs={{0,254},{2,0},{4,2},{6,4},{8,6},{10,8},{12,10},{14,12},{16,14},{18... | collective-permute-start | bytes 786440 | tf_op jit(solution)/shard_map/ppermute | solution.py:23
  33.0 15.4 %copy-start.3 = (f32[8192]{0:T(1024)S(1)}, f32[8192]{0:T(1024)}, u32[]{:S(2)}) copy-start(f32[8192]{0:T(1024)} %param.11) | copy-start | bytes 98308
  48.4 2.8 copy-start.1
where the time goes:
time: 406 us; the launch traced here: 405 us
  blocking collectives  350 us (86%)
  matrix products  30.1 us (7%)
  starting transfers between devices  11 us (3%)
  other arithmetic  8 us (2%)
  local copies, waits for them, and re-layouts  5.13 us (1%)
    psum x1, blocking collectives, on_device(): target_ocean, got_ocean = lax.psum((target_ocean, got_ocean), 'curve')  350 us
    dot_general x1, matrix products, slot_terms(): jnp.einsum('tij,ftj->fti', weights, source_blocks[:, slot_cols, :], preci...  15.4 us
    dot_general x1, matrix products, slot_terms(): jnp.einsum('tij,fti->ftj', weights, weighted_blocks[:, slot_rows, :], pre...  9.54 us
    ppermute x2, starting transfers between devices, from_behind(): lax.ppermute(shard, axis, [(i, (i + by) % size) for i in range(size)])  8.77 us
  transfers between devices with their start and end apart: 4, of which 0 were waited for; matrix products, arithmetic and copies ran while one was open for 9% of the time, Pallas kernels for 0%

commit v1 on v0

--- a/solution.py
+++ b/solution.py
@@ -1,6 +1,10 @@
+import functools
+
 import jax
 import jax.numpy as jnp
 from jax import lax
+from jax.experimental import pallas as pl
+from jax.experimental.pallas import tpu as pltpu
 from jax.sharding import PartitionSpec as P
 
 
@@ -53,6 +57,68 @@
     return (ocean_part, window_part)
 
 
+PLANE = 16
+MESH = pl.DeviceIdType.MESH
+
+
+def sum_kernel(layers, mine, out, work, got_plane, got_line, send_plane, recv_plane, send_line, recv_line):
+    me = lax.axis_index("curve")
+    core = lax.axis_index("field")
+    layer, place = me // PLANE, me % PLANE
+
+    def plane_partner(k):
+        return (layer * PLANE + (place + k) % PLANE, core)
+
+    def line_partner(k):
+        return ((layer + k) % layers * PLANE + place, core)
+
+    barrier = pltpu.get_barrier_semaphore()
+    for k in range(1, PLANE):
+        pl.semaphore_signal(barrier, inc=1, device_id=plane_partner(k), device_id_type=MESH)
+    for k in range(1, layers):
+        pl.semaphore_signal(barrier, inc=1, device_id=line_partner(k), device_id_type=MESH)
+    pl.semaphore_wait(barrier, PLANE + layers - 2)
+
+    def exchange(source, count, partner, landed, send, recv):
+        for k in range(1, count):
+            pltpu.make_async_remote_copy(
+                src_ref=source,
+                dst_ref=landed.at[k - 1],
+                send_sem=send,
+                recv_sem=recv,
+                device_id=partner(k),
+                device_id_type=MESH,
+            ).start()
+        pltpu.make_async_copy(landed, landed, recv).wait()
+
+    exchange(mine, PLANE, plane_partner, got_plane, send_plane, recv_plane)
+    work[...] = mine[...] + jnp.sum(got_plane[...], axis=0)
+    exchange(work, layers, line_partner, got_line, send_line, recv_line)
+    out[...] = work[...] + jnp.sum(got_line[...], axis=0)
+    pltpu.make_async_copy(got_plane, got_plane, send_plane).wait()
+    pltpu.make_async_copy(got_line, got_line, send_line).wait()
+
+
+def sum_all(values):
+    layers = lax.axis_size("curve") // PLANE
+    return pl.pallas_call(
+        functools.partial(sum_kernel, layers),
+        out_shape=jax.ShapeDtypeStruct(values.shape, jnp.float32),
+        in_specs=[pl.BlockSpec(memory_space=pltpu.VMEM)],
+        out_specs=pl.BlockSpec(memory_space=pltpu.VMEM),
+        scratch_shapes=[
+            pltpu.VMEM(values.shape, jnp.float32),
+            pltpu.VMEM((PLANE - 1, *values.shape), jnp.float32),
+            pltpu.VMEM((layers - 1, *values.shape), jnp.float32),
+            pltpu.SemaphoreType.DMA,
+            pltpu.SemaphoreType.DMA,
+            pltpu.SemaphoreType.DMA,
+            pltpu.SemaphoreType.DMA,
+        ],
+        compiler_params=pltpu.CompilerParams(collective_id=0, has_side_effects=True),
+    )(values)
+
+
 def on_device(atm_flux, ocean_state, area_atm, area_ocean, tiles, tile_row, tile_col, tile_count):
     local_fields, atm_cells = atm_flux.shape
     slot_cap, block_size = (tiles.shape[0], tiles.shape[1])
@@ -85,7 +151,6 @@
     target_ocean = jnp.sum(atm_flux * area_atm[None, :], axis=1)
     got_ocean = jnp.sum(ocean_remap * area_ocean[None, :], axis=1)
     target_atm = jnp.sum(ocean_state * area_ocean[None, :], axis=1)
-    target_ocean, got_ocean = lax.psum((target_ocean, got_ocean), "curve")
     window_flat = window_part.reshape(local_fields, window_span * block_size)
     rim_cells = margin_blocks * block_size
     core_cells = atm_span * block_size
@@ -97,7 +162,8 @@
     back_sum = core_part + jnp.pad(from_below, ((0, 0), (0, core_cells - rim_cells)))
     back_sum = back_sum + jnp.pad(from_above, ((0, 0), (core_cells - rim_cells, 0)))
     got_atm = jnp.sum(back_sum, axis=1)
-    target_atm, got_atm = lax.psum((target_atm, got_atm), "curve")
+    sums = jnp.stack([target_ocean, got_ocean, target_atm, got_atm])
+    target_ocean, got_ocean, target_atm, got_atm = sum_all(jnp.pad(sums, ((0, 4), (0, 96))))[:4, :local_fields]
     ocean_flux = ocean_remap * (target_ocean / got_ocean)[:, None]
     atm_fixed = back_sum / area_atm[None, :] * (target_atm / got_atm)[:, None]
     return (ocean_flux, atm_fixed)

time: 406 us -> 79.1 us (0.19)
  blocking collectives: 350 us -> 0 us
  Pallas kernels: 0 us -> 22.3 us
    psum x1 -> x0, blocking collectives: 350 us -> none  [on_device(): target_ocean, got_ocean = lax.psum((target_ocean, got_ocean), 'curve')]
    pallas_call x0 -> x1, Pallas kernels: none -> 22.3 us  [sum_all(): pl.pallas_call(functools.partial(sum_kernel, layers), out_shape=jax.Shape...]
  transfers between devices with their start and end apart: 4 -> 4, of which waited for: 0 -> 0; matrix products, arithmetic and copies ran while one was open for 9% -> 46% of each run, Pallas kernels for 0% -> 0%
where the time goes in v1:
time: 79.1 us; the launch traced here: 78.8 us
  matrix products  30.1 us (38%)
  Pallas kernels  22.3 us (28%)
  starting transfers between devices  11 us (14%)
  other arithmetic  8.77 us (11%)
  local copies, waits for them, and re-layouts  5.13 us (6%)
  between operations  1.51 us (2%)
    pallas_call x1, Pallas kernels, sum_all(): pl.pallas_call(functools.partial(sum_kernel, layers), out_shape=jax.Shape...  22.3 us
    dot_general x1, matrix products, slot_terms(): jnp.einsum('tij,ftj->fti', weights, source_blocks[:, slot_cols, :], preci...  15.4 us
    dot_general x1, matrix products, slot_terms(): jnp.einsum('tij,fti->ftj', weights, weighted_blocks[:, slot_rows, :], pre...  9.54 us
    ppermute x2, starting transfers between devices, from_behind(): lax.ppermute(shard, axis, [(i, (i + by) % size) for i in range(size)])  8.77 us
    dot_general x1, matrix products, slot_terms(): jnp.einsum('to,fti->foi', row_onehot, forward, precision=exact_mode)  2.72 us
    dot_general x1, matrix products, slot_terms(): jnp.einsum('tw,ftj->fwj', col_onehot, backward, precision=exact_mode)  2.49 us
    ppermute x1, starting transfers between devices, with_halo(): lax.ppermute(lax.slice_in_dim(block, 0, width, axis=dim), axis, backward)  2.19 us
    slice x1, local copies, waits for them, and re-layouts, with_halo(): lax.slice_in_dim(block, block.shape[dim] - width, None, axis=dim)  1.85 us
  transfers between devices with their start and end apart: 4, of which 0 were waited for; matrix products, arithmetic and copies ran while one was open for 46% of the time, Pallas kernels for 0%

profile of v1, /device:TPU:8, one launch (start us, length us, event | category | flops | bytes accessed | tf_op | source)
XLA Modules:
  0.0 78.8 jit_solution(7916278889175401721)
XLA Ops:
  0.6 1.9 %fusion.33 = (f32[32,2048]{1,0:T(8,128)}, f32[32,2048]{1,0:T(8,128)}) fusion(f32[32,4096]{1,0:T(8,128)} %param.8), kind=kLoop, calls=%fused_computation.60 | loop fusion | bytes 1048576 | tf_op jit(solution)/shard_map/slice | solution.py:18
  2.5 2.2 %collective-permute-start.1 = (f32[32,2048]{1,0:T(8,128)}, f32[32,2048]{1,0:T(8,128)}, u32[]{:S(2)}, u32[]{:S(2)}) collective-permute-start(f32[32,2048]{1,0:T(8,128)} %get-tuple-element.11), channel_id=1, source_target_pairs={{2,0},{4,2},{6,4},{8,6},{10,8},{12,10},{14,12},{16,14},{18,16},{20... | collective-permute-start | bytes 786440 | tf_op jit(solution)/shard_map/ppermute | solution.py:20
  5.3 0.0 copy-start.5
  5.4 0.0 copy-start.6
  5.4 1.4 %multiply_reduce_fusion = (f32[32]{0:T(128)S(1)}, f32[4,64,8,128]{3,2,1,0:T(8,128)S(1)}) fusion(f32[32,8192]{1,0:T(8,128)} %param.9, f32[8192]{0:T(1024)} %param.11), kind=kLoop, calls=%fused_computation.20 | loop fusion | flops 524256 | bytes 2130048 | tf_op jit(solution)/shard_map/reduce_sum | solution.py:153
  6.8 0.1 copy.29
  7.0 0.8 %gather_fusion.1 = f32[128,32,128]{2,1,0:T(8,128)S(1)} fusion(f32[32,64,128]{2,0,1:T(8,128)S(1)} %bitcast.57, s32[1024]{0:T(1024)S(1)} %pad_clamp_fusion), kind=kCustom, calls=%fused_computation.1 | custom fusion | bytes 4194816 | tf_op jit(solution)/shard_map/gather | solution.py:50
  7.8 9.5 %fusion.11 = f32[32,128,128]{2,0,1:T(8,128)S(1)} fusion(f32[128,128,128]{2,1,0:T(8,128)} %param.12, f32[128,32,128]{2,1,0:T(8,128)S(1)} %gather_fusion.1), kind=kOutput, calls=%fused_computation.11 | convolution fusion | flops 805306368 | bytes 12582912 | tf_op jit(solution)/shard_map/tij,fti->ftj/dot_general | solution.py:49
  17.3 2.5 %fusion.4 = f32[32,128,64]{1,2,0:T(8,128)S(1)} fusion(f32[32,128,128]{2,0,1:T(8,128)S(1)} %fusion.11, s32[128]{0:T(128)S(1)} %get-tuple-element.5, f32[128]{0:T(128)S(1)} %compare_convert_fusion), kind=kOutput, calls=%fused_computation.6 | convolution fusion | flops 402669568 | bytes 3146752 | tf_op jit(solution)/shard_map/tw,ftj->fwj/dot_general | solution.py:56
  19.9 0.6 copy.28
  20.5 0.0 copy-start
  20.5 0.9 %fusion.32 = (f32[32,2048]{1,0:T(8,128)}, f32[32,2048]{1,0:T(8,128)}) fusion(f32[32,8192]{1,0:T(8,128)S(1)} %bitcast.58), kind=kLoop, calls=%fused_computation.59 | loop fusion | bytes 1048576 | tf_op jit(solution)/shard_map/slice | solution.py:158
  21.4 8.8 %collective-permute-start.3 = (f32[32,2048]{1,0:T(8,128)}, f32[32,2048]{1,0:T(8,128)S(1)}, u32[]{:S(2)}, u32[]{:S(2)}) collective-permute-start(f32[32,2048]{1,0:T(8,128)} %get-tuple-element.9), channel_id=1, source_target_pairs={{0,254},{2,0},{4,2},{6,4},{8,6},{10,8},{12,10},{14,12},{16,14},{18... | collective-permute-start | bytes 786440 | tf_op jit(solution)/shard_map/ppermute | solution.py:27
  30.2 0.2 multiply_reduce_fusion.1
  30.4 1.2 %copy_bitcast_fusion.2 = f32[32,64,128]{2,0,1:T(8,128)S(1)} fusion(f32[32,2048]{1,0:T(8,128)} %collective-permute-done.1, f32[32,4096]{1,0:T(8,128)S(1)} %copy-done.2, f32[32,2048]{1,0:T(8,128)} %collective-permute-done), kind=kLoop, calls=%fused_computation.15 | loop fusion | flops 524288 | bytes 2097152 | tf_op jit(solution)/shard_map/reshape | solution.py:132
  31.6 0.8 %gather_fusion = f32[128,32,128]{2,1,0:T(8,128)S(1)} fusion(f32[32,64,128]{2,0,1:T(8,128)S(1)} %copy_bitcast_fusion.2, s32[1024]{0:T(1024)S(1)} %pad_clamp_fusion.1), kind=kCustom, calls=%fused_computation | custom fusion | bytes 4194816 | tf_op jit(solution)/shard_map/gather | solution.py:42
  32.4 15.4 %fusion.8 = f32[32,128,128]{2,0,1:T(8,128)S(1)} fusion(f32[128,128,128]{2,1,0:T(8,128)} %param.12, f32[128,32,128]{2,1,0:T(8,128)S(1)} %gather_fusion), kind=kOutput, calls=%fused_computation.10 | convolution fusion | flops 805306368 | bytes 12582912 | tf_op jit(solution)/shard_map/tij,ftj->fti/dot_general | solution.py:41
  47.8 2.7 %fusion.14 = (f32[32]{0:T(128)S(1)}, f32[32,128,64]{1,2,0:T(8,128)S(1)}) fusion(f32[64,128]{1,0:T(8,128)S(1)} %bitcast.63, f32[128]{0:T(128)S(1)} %compare_convert_fusion, s32[128]{0:T(128)S(1)} %get-tuple-element.3, f32[32,128,128]{2,0,1:T(8,128)S(1)} %fusion.8), kind=kOutput, calls=%fused_computation.18 | convolution fusion | flops 403193824 | bytes 3179648 | tf_op jit(solution)/shard_map/to,fti->foi/dot_general | solution.py:48
  50.5 1.1 %fusion.16 = f32[32]{0:T(128)S(1)} fusion(f32[32,2048]{1,0:T(8,128)S(1)} %collective-permute-done.3, f32[32,2048]{1,0:T(8,128)} %collective-permute-done.2, f32[32,8192]{1,0:T(8,128)S(1)} %bitcast.59), kind=kLoop, calls=%fused_computation.25 | loop fusion | flops 393184 | bytes 1048704 | tf_op jit(solution)/shard_map/reduce_sum | solution.py:164
  51.6 0.6 select_maximum_fusion.mine
  52.2 22.3 %shard_map.95 = f32[8,128]{1,0:T(8,128)} custom-call(f32[8,128]{1,0:T(8,128)} %select_maximum_fusion.mine), custom_call_target="tpu_custom_call" | custom-call | tf_op jit(solution)/shard_map/pallas_call | solution.py:104
  74.5 0.8 %fusion.29 = (f32[32]{0:T(128)S(1)}, f32[32]{0:T(128)S(1)}) fusion(f32[8,128]{1,0:T(8,128)} %shard_map.95), kind=kLoop, calls=%fused_computation.55 | loop fusion | flops 64 | bytes 768 | tf_op jit(solution)/shard_map/div | solution.py:168
  75.3 1.6 %bitcast_multiply_fusion = f32[32,8192]{1,0:T(8,128)} fusion(f32[4,8,64,128]{3,2,1,0:T(8,128)S(1)} %bitcast.61, f32[32]{0:T(128)S(1)} %get-tuple-element.13), kind=kLoop, calls=%fused_computation.13 | loop fusion | flops 262144 | bytes 2097280 | tf_op jit(solution)/shard_map/mul | solution.py:167
  76.9 1.8 %divide_multiply_fusion = f32[32,4096]{1,0:T(8,128)} fusion(f32[32]{0:T(128)S(1)} %get-tuple-element.12, f32[4096]{0:T(1024)S(1)} %copy-done.4, f32[32,2048]{1,0:T(8,128)S(1)} %collective-permute-done.3, f32[32,2048]{1,0:T(8,128)} %collective-permute-done.2, f32[32,8192]{1,0:T(8,128)S(1)} %bitcast.60), kind=kLoop, calls=%fused_computation.23 | loop fusion | flops 524288 | bytes 1589376 | tf_op jit(solution)/shard_map/mul | solution.py:168
  (22 shorter events, 0.1 us)
Async XLA Ops:
  2.5 27.9 %collective-permute-start.1 = (f32[32,2048]{1,0:T(8,128)}, f32[32,2048]{1,0:T(8,128)}, u32[]{:S(2)}, u32[]{:S(2)}) collective-permute-start(f32[32,2048]{1,0:T(8,128)} %get-tuple-element.11), channel_id=1, source_target_pairs={{2,0},{4,2},{6,4},{8,6},{10,8},{12,10},{14,12},{16,14},{18,16},{20... | collective-permute-start | bytes 786440 | tf_op jit(solution)/shard_map/ppermute | solution.py:20
  4.7 25.7 %collective-permute-start = (f32[32,2048]{1,0:T(8,128)}, f32[32,2048]{1,0:T(8,128)}, u32[]{:S(2)}, u32[]{:S(2)}) collective-permute-start(f32[32,2048]{1,0:T(8,128)} %get-tuple-element.10), channel_id=1, source_target_pairs={{0,2},{2,4},{4,6},{6,8},{8,10},{10,12},{12,14},{14,16},{16,18},{18... | collective-permute-start | bytes 786440 | tf_op jit(solution)/shard_map/ppermute | solution.py:17
  5.3 1.6 %copy-start.5 = (s32[128]{0:T(128)S(1)}, s32[128]{0:T(128)}, u32[]{:S(2)}) copy-start(s32[128]{0:T(128)} %param.13) | copy-start | bytes 1540
  5.4 1.6 %copy-start.6 = (s32[128]{0:T(128)S(1)}, s32[128]{0:T(128)}, u32[]{:S(2)}) copy-start(s32[128]{0:T(128)} %param.14) | copy-start | bytes 1540
  19.8 10.3 %copy-start.2 = (f32[32,4096]{1,0:T(8,128)S(1)}, f32[32,4096]{1,0:T(8,128)}, u32[]{:S(2)}) copy-start(f32[32,4096]{1,0:T(8,128)} %param.8) | copy-start | bytes 1572868
  19.9 10.3 %copy-start.4 = (f32[4096]{0:T(1024)S(1)}, f32[4096]{0:T(1024)}, u32[]{:S(2)}) copy-start(f32[4096]{0:T(1024)} %param.10) | copy-start | bytes 49156
  20.5 9.9 %copy-start = (f32[4,8,64,128]{3,1,2,0:T(8,128)}, f32[4,8,64,128]{3,1,2,0:T(8,128)S(1)}, u32[]{:S(2)}) copy-start(f32[4,8,64,128]{3,1,2,0:T(8,128)S(1)} %copy.28) | copy-start | bytes 3145732
  21.4 29.1 %collective-permute-start.3 = (f32[32,2048]{1,0:T(8,128)}, f32[32,2048]{1,0:T(8,128)S(1)}, u32[]{:S(2)}, u32[]{:S(2)}) collective-permute-start(f32[32,2048]{1,0:T(8,128)} %get-tuple-element.9), channel_id=1, source_target_pairs={{0,254},{2,0},{4,2},{6,4},{8,6},{10,8},{12,10},{14,12},{16,14},{18... | collective-permute-start | bytes 786440 | tf_op jit(solution)/shard_map/ppermute | solution.py:27
  30.2 20.3 %collective-permute-start.2 = (f32[32,2048]{1,0:T(8,128)}, f32[32,2048]{1,0:T(8,128)}, u32[]{:S(2)}, u32[]{:S(2)}) collective-permute-start(f32[32,2048]{1,0:T(8,128)} %get-tuple-element.8), channel_id=1, source_target_pairs={{0,2},{2,4},{4,6},{6,8},{8,10},{10,12},{12,14},{14,16},{16,18},{18... | collective-permute-start | bytes 786440 | tf_op jit(solution)/shard_map/ppermute | solution.py:27
  32.4 15.4 %copy-start.3 = (f32[8192]{0:T(1024)S(1)}, f32[8192]{0:T(1024)}, u32[]{:S(2)}) copy-start(f32[8192]{0:T(1024)} %param.11) | copy-start | bytes 98308
  47.8 2.8 %copy-start.1 = (f32[4,8,64,128]{3,1,2,0:T(8,128)S(1)}, f32[4,8,64,128]{3,1,2,0:T(8,128)}, u32[]{:S(2)}) copy-start(f32[4,8,64,128]{3,1,2,0:T(8,128)} %copy-done) | copy-start | bytes 3145732

commit v2 on v0

v2 whole, which is shorter than its diff:
```python
import functools

import jax
import jax.numpy as jnp
from jax import lax
from jax.experimental import pallas as pl
from jax.experimental.pallas import tpu as pltpu
from jax.sharding import PartitionSpec as P

MESH = pl.DeviceIdType.MESH
LANES = 128
CHUNK = 16
GROUP = 8
MIB = 1024 * 1024


def split(values):
    high = values.astype(jnp.bfloat16)
    return high, (values - high.astype(jnp.float32)).astype(jnp.bfloat16)


def twice(block):
    return jnp.concatenate([block, block], axis=1)


def lane_block(index):
    return pl.ds(pl.multiple_of(index * LANES, LANES), LANES)


def remap_kernel(
    flux,
    state,
    area_atm,
    area_ocean,
    tiles,
    tile_row,
    tile_col,
    tile_count,
    ocean_out,
    atm_out,
    sums_out,
    flux_own,
    flux_low,
    flux_high,
    state_own,
    tiles_own,
    tiles_split,
    state_split,
    flux_split,
    back_chain,
    ocean_chain,
    back_core,
    send_low,
    send_high,
    got_low,
    got_high,
    ones_back,
    ocean_own,
    table,
    index,
    mine,
    landed,
    total,
    load_sem,
    tile_sem,
    index_sem,
    store_sem,
    flux_send_sem,
    flux_recv_sem,
    back_send_sem,
    back_recv_sem,
    sum_send_sem,
    sum_recv_sem,
):
    count = lax.axis_size("curve")
    me = lax.axis_index("curve")
    core = lax.axis_index("field")
    above = (lax.rem(me + 1, count), core)
    below = (lax.rem(me + count - 1, count), core)
    fields, atm_cells = flux.shape
    ocean_cells = state.shape[1]
    slots = tiles.shape[0]
    atm_span, ocean_span = atm_cells // LANES, ocean_cells // LANES
    margin = atm_span // 2
    window_span = atm_span + 2 * margin
    rim = margin * LANES

    def partner(step):
        away = (step + 1) // 2
        shift = jnp.where(step % 2 == 0, away, -away)
        return (lax.rem(me + count // 2 + shift + count, count), core)

    barrier = pltpu.get_barrier_semaphore()

    def greet(step, carry):
        pl.semaphore_signal(barrier, inc=1, device_id=partner(step), device_id_type=MESH)
        return carry

    lax.fori_loop(0, count - 1, greet, 0)

    load_state = pltpu.make_async_copy(state, state_own, load_sem.at[0])
    load_flux = pltpu.make_async_copy(flux, flux_own, load_sem.at[1])
    load_state.start()
    load_flux.start()
    chunks = slots // CHUNK

    def load_tiles(chunk):
        part = pl.ds(chunk * CHUNK, CHUNK)
        return pltpu.make_async_copy(tiles.at[part], tiles_own.at[part], tile_sem.at[chunk])

    for chunk in range(chunks):
        load_tiles(chunk).start()

    slot_of_row = lax.broadcasted_iota(jnp.int32, (slots, LANES), 0)
    lane = lax.broadcasted_iota(jnp.int32, (slots, LANES), 1)
    live = slot_of_row < tile_count[0]

    def chain_of(names):
        across = jnp.broadcast_to(names, (slots, LANES))
        down = jnp.transpose(across.astype(jnp.float32)).astype(jnp.int32)
        former = jnp.where((across == down) & (slot_of_row < lane), slot_of_row + 1, 0)
        last = jnp.where((lane == down) & live, slot_of_row + 1, 0)
        return jnp.max(former, axis=0, keepdims=True), jnp.max(last, axis=0, keepdims=True)

    row_names = tile_row[...] - me * ocean_span
    col_names = tile_col[...] - me * atm_span + margin
    ring = atm_span * count
    col_names = jnp.where(col_names < 0, col_names + ring, col_names)
    col_names = jnp.where(col_names >= ring, col_names - ring, col_names)
    row_names = jnp.clip(row_names, 0, ocean_span - 1)
    col_names = jnp.clip(col_names, 0, window_span - 1)
    row_former, row_last = chain_of(row_names)
    col_former, col_last = chain_of(col_names)
    for place, row in enumerate(
        (row_names, col_names, row_former, row_last, col_former, col_last)
    ):
        table[place : place + 1, :] = row
    table[6:8, :] = jnp.zeros((2, LANES), jnp.int32)
    index_copy = pltpu.make_async_copy(table, index, index_sem)
    index_copy.start()

    pl.semaphore_wait(barrier, count - 1)

    def remote(source, target, sends, receives, place, device):
        return pltpu.make_async_remote_copy(
            src_ref=source,
            dst_ref=target,
            send_sem=sends.at[place],
            recv_sem=receives.at[place],
            device_id=device,
            device_id_type=MESH,
        )

    flux_up = remote(
        flux.at[:, pl.ds(atm_cells - rim, rim)], flux_low, flux_send_sem, flux_recv_sem, 0, above
    )
    flux_down = remote(flux.at[:, pl.ds(0, rim)], flux_high, flux_send_sem, flux_recv_sem, 1, below)
    flux_up.start()
    flux_down.start()

    zeros = jnp.zeros((fields, LANES), jnp.float32)
    extra = lax.broadcasted_iota(jnp.int32, (16, LANES), 0)
    load_state.wait()

    def weigh(block, acc):
        area = area_ocean[:, lane_block(block)]
        weighted = state_own[:, lane_block(block)] * area
        high, low = split(weighted)
        state_split[block, 0:fields, :] = high
        state_split[block, fields : 2 * fields, :] = low
        area_high = area.astype(jnp.bfloat16).astype(jnp.float32)
        area_rows = jnp.where(
            extra == 0, area_high, jnp.where(extra == 1, area - area_high, 0.0)
        )
        state_split[block, 2 * fields : 2 * fields + 16, :] = area_rows.astype(jnp.bfloat16)
        return acc + weighted

    target_atm = lax.fori_loop(0, ocean_span, weigh, zeros)

    back_chain[0] = jnp.zeros(back_chain.shape[1:], jnp.float32)
    ocean_chain[0] = jnp.zeros(ocean_chain.shape[1:], jnp.float32)
    index_copy.wait()

    def backward(step, carry):
        for part in range(GROUP):
            slot = step * GROUP + part
            high, low = split(tiles_own[slot])
            tiles_split[slot, 0] = high
            tiles_split[slot, 1] = low
            terms = jnp.dot(
                twice(state_split[index[0, slot]]),
                jnp.concatenate([high, low], axis=0),
                preferred_element_type=jnp.float32,
            )
            former = index[4, slot]
            back_chain[slot + 1, 0:fields, :] = (
                terms[0:fields] + terms[fields : 2 * fields] + back_chain[former, 0:fields, :]
            )
            back_chain[slot + 1, fields : fields + 8, :] = (
                terms[2 * fields : 2 * fields + 8] + back_chain[former, fields : fields + 8, :]
            )
        return carry

    steps = CHUNK // GROUP
    for chunk in range(chunks):
        load_tiles(chunk).wait()
        lax.fori_loop(chunk * steps, (chunk + 1) * steps, backward, 0)

    def collect(target, first):
        def one(block, acc):
            slot = index[5, first + block]
            sums = back_chain[slot, 0:fields, :]
            target[:, lane_block(block)] = sums
            ones_back[first + block] = jnp.sum(
                back_chain[slot, fields : fields + 8, :], axis=0, keepdims=True
            )
            return acc + sums

        return one

    got_atm = lax.fori_loop(0, margin, collect(send_low, 0), zeros)
    back_down = remote(send_low, got_high, back_send_sem, back_recv_sem, 1, below)
    back_down.start()
    got_atm = lax.fori_loop(0, margin, collect(send_high, margin + atm_span), got_atm)
    back_up = remote(send_high, got_low, back_send_sem, back_recv_sem, 0, above)
    back_up.start()
    got_atm = lax.fori_loop(0, atm_span, collect(back_core, margin), got_atm)

    load_flux.wait()

    def spread(source, first, own):
        def one(block, acc):
            values = source[:, lane_block(block)]
            high, low = split(values)
            flux_split[first + block, 0:fields, :] = high
            flux_split[first + block, fields : 2 * fields, :] = low
            got = acc[1] + values * ones_back[first + block]
            if own:
                return acc[0] + values * area_atm[:, lane_block(block)], got
            return acc[0], got

        return one

    acc = lax.fori_loop(0, atm_span, spread(flux_own, margin, True), (zeros, zeros))
    flux_up.wait_recv()
    flux_down.wait_recv()
    acc = lax.fori_loop(0, margin, spread(flux_low, 0, False), acc)
    target_ocean, got_ocean = lax.fori_loop(
        0, margin, spread(flux_high, margin + atm_span, False), acc
    )

    stacked = jnp.concatenate([target_ocean, got_ocean, target_atm, got_atm], axis=0)
    mine[...] = jnp.sum(jnp.transpose(stacked), axis=0, keepdims=True)

    def send_row(step, carry):
        pltpu.make_async_remote_copy(
            src_ref=mine,
            dst_ref=landed.at[step],
            send_sem=sum_send_sem,
            recv_sem=sum_recv_sem,
            device_id=partner(step),
            device_id_type=MESH,
        ).start()
        return carry

    lax.fori_loop(0, count - 1, send_row, 0)

    def forward(step, carry):
        for part in range(GROUP):
            slot = step * GROUP + part
            terms = lax.dot_general(
                twice(flux_split[index[1, slot]]),
                jnp.concatenate([tiles_split[slot, 0], tiles_split[slot, 1]], axis=1),
                (((1,), (1,)), ((), ())),
                preferred_element_type=jnp.float32,
            )
            ocean_chain[slot + 1] = (
                terms[0:fields] + terms[fields : 2 * fields] + ocean_chain[index[2, slot]]
            )
        return carry

    lax.fori_loop(0, slots // GROUP, forward, 0)

    def place_ocean(block, carry):
        ocean_own[:, lane_block(block)] = ocean_chain[index[3, block]]
        return carry

    lax.fori_loop(0, ocean_span, place_ocean, 0)
    store_ocean = pltpu.make_async_copy(ocean_own, ocean_out, store_sem.at[0])
    store_ocean.start()

    back_up.wait_recv()
    back_down.wait_recv()
    half = atm_cells - rim
    back_core[:, 0:rim] = (back_core[:, 0:rim] + got_low[...]) / area_atm[:, 0:rim]
    back_core[:, half:] = (back_core[:, half:] + got_high[...]) / area_atm[:, half:]
    store_atm = pltpu.make_async_copy(back_core, atm_out, store_sem.at[1])
    store_atm.start()

    pltpu.make_async_copy(landed, landed, sum_recv_sem).wait()
    total[...] = mine[...] + jnp.sum(landed[...], axis=0)
    store_sums = pltpu.make_async_copy(total, sums_out, store_sem.at[2])
    store_sums.start()
    for copy in (flux_up, flux_down, back_up, back_down):
        copy.wait_send()
    pltpu.make_async_copy(landed, landed, sum_send_sem).wait()
    store_ocean.wait()
    store_atm.wait()
    store_sums.wait()


def scale_kernel(ocean, atm, sums, ocean_out, atm_out):
    fields = ocean.shape[0]
    columns = jnp.transpose(jnp.broadcast_to(sums[...], (LANES, LANES)))
    target_ocean, got_ocean, target_atm, got_atm = (
        columns[part * fields : (part + 1) * fields, 0:1] for part in range(4)
    )
    ocean_out[...] = ocean[...] * (target_ocean / got_ocean)
    atm_out[...] = atm[...] * (target_atm / got_atm)


def on_device(atm_flux, ocean_state, area_atm, area_ocean, tiles, tile_row, tile_col, tile_count):
    fields, atm_cells = atm_flux.shape
    ocean_cells = ocean_state.shape[1]
    slots = tiles.shape[0]
    devices = lax.axis_size("curve")
    atm_span, ocean_span = atm_cells // LANES, ocean_cells // LANES
    margin = atm_span // 2
    window_span = atm_span + 2 * margin
    rim = margin * LANES
    f32, bf16 = jnp.float32, jnp.bfloat16
    anywhere = pl.BlockSpec(memory_space=pl.ANY)
    vmem = pl.BlockSpec(memory_space=pltpu.VMEM)
    smem = pl.BlockSpec(memory_space=pltpu.SMEM)
    ocean_raw, atm_raw, sums = pl.pallas_call(
        remap_kernel,
        out_shape=(
            jax.ShapeDtypeStruct((fields, ocean_cells), f32),
            jax.ShapeDtypeStruct((fields, atm_cells), f32),
            jax.ShapeDtypeStruct((1, LANES), f32),
        ),
        in_specs=[anywhere, anywhere, vmem, vmem, anywhere, vmem, vmem, smem],
        out_specs=(anywhere, anywhere, anywhere),
        scratch_shapes=[
            pltpu.VMEM((fields, atm_cells), f32),
            pltpu.VMEM((fields, rim), f32),
            pltpu.VMEM((fields, rim), f32),
            pltpu.VMEM((fields, ocean_cells), f32),
            pltpu.VMEM(tiles.shape, f32),
            pltpu.VMEM((slots, 2, LANES, LANES), bf16),
            pltpu.VMEM((ocean_span, 2 * fields + 16, LANES), bf16),
            pltpu.VMEM((window_span, 2 * fields, LANES), bf16),
            pltpu.VMEM((slots + 1, fields + 8, LANES), f32),
            pltpu.VMEM((slots + 1, fields, LANES), f32),
            pltpu.VMEM((fields, atm_cells), f32),
            pltpu.VMEM((fields, rim), f32),
            pltpu.VMEM((fields, rim), f32),
            pltpu.VMEM((fields, rim), f32),
            pltpu.VMEM((fields, rim), f32),
            pltpu.VMEM((window_span, 1, LANES), f32),
            pltpu.VMEM((fields, ocean_cells), f32),
            pltpu.VMEM((8, LANES), jnp.int32),
            pltpu.SMEM((8, LANES), jnp.int32),
            pltpu.VMEM((1, LANES), f32),
            pltpu.VMEM((devices - 1, 1, LANES), f32),
            pltpu.VMEM((1, LANES), f32),
            pltpu.SemaphoreType.DMA((2,)),
            pltpu.SemaphoreType.DMA((slots // CHUNK,)),
            pltpu.SemaphoreType.DMA,
            pltpu.SemaphoreType.DMA((3,)),
            pltpu.SemaphoreType.DMA((2,)),
            pltpu.SemaphoreType.DMA((2,)),
            pltpu.SemaphoreType.DMA((2,)),
            pltpu.SemaphoreType.DMA((2,)),
            pltpu.SemaphoreType.DMA,
            pltpu.SemaphoreType.DMA,
        ],
        compiler_params=pltpu.CompilerParams(
            collective_id=0, has_side_effects=True, vmem_limit_bytes=48 * MIB
        ),
        name="remap",
    )(
        atm_flux,
        ocean_state,
        area_atm.reshape(1, atm_cells),
        area_ocean.reshape(1, ocean_cells),
        tiles,
        tile_row.reshape(1, slots),
        tile_col.reshape(1, slots),
        tile_count,
    )
    return pl.pallas_call(
        scale_kernel,
        grid=(4,),
        out_shape=(
            jax.ShapeDtypeStruct((fields, ocean_cells), f32),
            jax.ShapeDtypeStruct((fields, atm_cells), f32),
        ),
        in_specs=[
            pl.BlockSpec((fields, ocean_cells // 4), lambda step: (0, step)),
            pl.BlockSpec((fields, atm_cells // 4), lambda step: (0, step)),
            pl.BlockSpec((1, LANES), lambda step: (0, 0)),
        ],
        out_specs=(
            pl.BlockSpec((fields, ocean_cells // 4), lambda step: (0, step)),
            pl.BlockSpec((fields, atm_cells // 4), lambda step: (0, step)),
        ),
        name="scale",
    )(ocean_raw, atm_raw, sums)


def solution(mesh):
    in_specs = (
        P("field", "curve"),
        P("field", "curve"),
        P("curve"),
        P("curve"),
        P("curve", None, None),
        P("curve"),
        P("curve"),
        P("curve"),
    )
    out_specs = (P("field", "curve"), P("field", "curve"))
    return jax.shard_map(
        on_device, mesh=mesh, in_specs=in_specs, out_specs=out_specs, check_vma=False
    )
```

time: 406 us -> 45 us (0.11)
  blocking collectives: 350 us -> 0 us
  Pallas kernels: 0 us -> 35.9 us
  matrix products: 30.1 us -> 0 us
  starting transfers between devices: 11 us -> 0 us
  other arithmetic: 8 us -> 0 us
    psum x1 -> x0, blocking collectives: 350 us -> none  [on_device(): target_ocean, got_ocean = lax.psum((target_ocean, got_ocean), 'curve')]
    pallas_call x0 -> x2, Pallas kernels: none -> 35.9 us  [the longest x1 32.1 us: on_device(): pl.pallas_call(remap_kernel, out_shape=(jax.ShapeDtypeStruct((fields, oce...]
    dot_general x4 -> x0, matrix products: 30.1 us -> none  [the longest x1 15.4 us: slot_terms(): jnp.einsum('tij,ftj->fti', weights, source_blocks[:, slot_cols, :], preci...]
    ppermute x4 -> x0, starting transfers between devices: 11 us -> none  [the longest x2 8.77 us: from_behind(): lax.ppermute(shard, axis, [(i, (i + by) % size) for i in range(size)])]
    unnamed x13 -> x18, local copies, waits for them, and re-layouts: 0.65 us -> 7.39 us
  transfers between devices with their start and end apart: 4 -> 0, of which waited for: 0 -> 0; matrix products, arithmetic and copies ran while one was open for 9% -> 0% of each run, Pallas kernels for 0% -> 0%
where the time goes in v2:
time: 45 us; the launch traced here: 44.6 us
  Pallas kernels  35.9 us (80%)
  local copies, waits for them, and re-layouts  7.39 us (16%)
  between operations  1.31 us (3%)
    pallas_call x1, Pallas kernels, on_device(): pl.pallas_call(remap_kernel, out_shape=(jax.ShapeDtypeStruct((fields, oce...  32.1 us
    unnamed x18, local copies, waits for them, and re-layouts  7.39 us
    pallas_call x1, Pallas kernels, on_device(): pl.pallas_call(scale_kernel, grid=(4,), out_shape=(jax.ShapeDtypeStruct((...  3.82 us

profile of v2, /device:TPU:8, one launch (start us, length us, event | category | flops | bytes accessed | tf_op | source)
XLA Modules:
  0.0 44.6 jit_solution(17959982772426416650)
XLA Ops:
  1.3 0.0 copy-start.1
  1.3 1.2 %copy-done.1 = f32[32,8192]{1,0:T(8,128)S(1)} copy-done((f32[32,8192]{1,0:T(8,128)S(1)}, f32[32,8192]{1,0:T(8,128)}, u32[]{:S(2)}) %copy-start.1) | copy-done | bytes 1048600
  2.5 0.0 copy-start.3
  2.5 1.0 %copy-done.3 = f32[32,4096]{1,0:T(8,128)S(1)} copy-done((f32[32,4096]{1,0:T(8,128)S(1)}, f32[32,4096]{1,0:T(8,128)}, u32[]{:S(2)}) %copy-start.3) | copy-done | bytes 524312
  3.5 0.0 copy-start.4
  3.5 0.8 %copy-done.4 = f32[8192]{0:T(1024)S(1)} copy-done((f32[8192]{0:T(1024)S(1)}, f32[8192]{0:T(1024)}, u32[]{:S(2)}) %copy-start.4) | copy-done | bytes 32792
  4.3 0.0 copy-start.5
  4.3 0.7 %copy-done.5 = f32[4096]{0:T(1024)S(1)} copy-done((f32[4096]{0:T(1024)S(1)}, f32[4096]{0:T(1024)}, u32[]{:S(2)}) %copy-start.5) | copy-done | bytes 16408
  5.0 0.0 copy-start.7
  5.0 0.7 %copy-done.7 = s32[128]{0:T(128)S(1)} copy-done((s32[128]{0:T(128)S(1)}, s32[128]{0:T(128)}, u32[]{:S(2)}) %copy-start.7) | copy-done | bytes 536
  5.7 0.0 copy-start.8
  5.7 0.7 %copy-done.8 = s32[128]{0:T(128)S(1)} copy-done((s32[128]{0:T(128)S(1)}, s32[128]{0:T(128)}, u32[]{:S(2)}) %copy-start.8) | copy-done | bytes 536
  6.3 32.1 %remap.1 = (f32[32,8192]{1,0:T(8,128)S(1)}, f32[32,4096]{1,0:T(8,128)S(1)}, f32[1,128]{1,0:T(1,128)S(1)}) custom-call(f32[32,4096]{1,0:T(8,128)S(1)} %copy-done.3, f32[32,8192]{1,0:T(8,128)S(1)} %copy-done.1, f32[1,4096]{1,0:T(1,128)S(1)} %bitcast.5, f32[1,8192]{1,0:T(1,128)S(1)} %bitcast.4, f32[128,128,128]{2,1,0:T(8,128)} %tiles.1, s32[1,128]{1,0:T(1,128)S(1)} %bitcast.6, ...), custom_call_target="tpu_custom_call" | custom-call | tf_op jit(solution)/shard_map/remap/pallas_call | solution.py:335
  38.4 0.0 copy-start
  38.4 1.0 %copy-done = f32[32,8192]{1,0:T(8,128)} copy-done((f32[32,8192]{1,0:T(8,128)}, f32[32,8192]{1,0:T(8,128)S(1)}, u32[]{:S(2)}) %copy-start) | copy-done | bytes 1048600
  39.4 0.0 copy-start.2
  39.4 0.8 %copy-done.2 = f32[32,4096]{1,0:T(8,128)} copy-done((f32[32,4096]{1,0:T(8,128)}, f32[32,4096]{1,0:T(8,128)S(1)}, u32[]{:S(2)}) %copy-start.2) | copy-done | bytes 524312
  40.2 0.0 copy-start.6
  40.2 0.6 %copy-done.6 = f32[1,128]{1,0:T(1,128)} copy-done((f32[1,128]{1,0:T(1,128)}, f32[1,128]{1,0:T(1,128)S(1)}, u32[]{:S(2)}) %copy-start.6) | copy-done | bytes 536
  40.8 3.8 %scale.1 = (f32[32,8192]{1,0:T(8,128)}, f32[32,4096]{1,0:T(8,128)}) custom-call(f32[32,8192]{1,0:T(8,128)} %copy-done, f32[32,4096]{1,0:T(8,128)} %copy-done.2, f32[1,128]{1,0:T(1,128)} %copy-done.6), custom_call_target="tpu_custom_call" | custom-call | tf_op jit(solution)/shard_map/scale/pallas_call | solution.py:392
Async XLA Ops:
  1.3 1.2 %copy-start.1 = (f32[32,8192]{1,0:T(8,128)S(1)}, f32[32,8192]{1,0:T(8,128)}, u32[]{:S(2)}) copy-start(f32[32,8192]{1,0:T(8,128)} %state.1) | copy-start | bytes 3145732
  2.5 1.0 %copy-start.3 = (f32[32,4096]{1,0:T(8,128)S(1)}, f32[32,4096]{1,0:T(8,128)}, u32[]{:S(2)}) copy-start(f32[32,4096]{1,0:T(8,128)} %flux.1) | copy-start | bytes 1572868
  3.5 0.8 %copy-start.4 = (f32[8192]{0:T(1024)S(1)}, f32[8192]{0:T(1024)}, u32[]{:S(2)}) copy-start(f32[8192]{0:T(1024)} %param.11) | copy-start | bytes 98308
  4.3 0.7 %copy-start.5 = (f32[4096]{0:T(1024)S(1)}, f32[4096]{0:T(1024)}, u32[]{:S(2)}) copy-start(f32[4096]{0:T(1024)} %param.10) | copy-start | bytes 49156
  5.0 0.7 %copy-start.7 = (s32[128]{0:T(128)S(1)}, s32[128]{0:T(128)}, u32[]{:S(2)}) copy-start(s32[128]{0:T(128)} %param.13) | copy-start | bytes 1540
  5.7 0.7 %copy-start.8 = (s32[128]{0:T(128)S(1)}, s32[128]{0:T(128)}, u32[]{:S(2)}) copy-start(s32[128]{0:T(128)} %param.14) | copy-start | bytes 1540
  38.4 1.0 %copy-start = (f32[32,8192]{1,0:T(8,128)}, f32[32,8192]{1,0:T(8,128)S(1)}, u32[]{:S(2)}) copy-start(f32[32,8192]{1,0:T(8,128)S(1)} %get-tuple-element.5.ocean) | copy-start | bytes 3145732
  39.4 0.8 %copy-start.2 = (f32[32,4096]{1,0:T(8,128)}, f32[32,4096]{1,0:T(8,128)S(1)}, u32[]{:S(2)}) copy-start(f32[32,4096]{1,0:T(8,128)S(1)} %get-tuple-element.6.atm) | copy-start | bytes 1572868
  40.2 0.6 %copy-start.6 = (f32[1,128]{1,0:T(1,128)}, f32[1,128]{1,0:T(1,128)S(1)}, u32[]{:S(2)}) copy-start(f32[1,128]{1,0:T(1,128)S(1)} %get-tuple-element.7.sums) | copy-start | bytes 1540

commit v3 on v2

--- a/solution.py
+++ b/solution.py
@@ -9,6 +9,7 @@
 
 MESH = pl.DeviceIdType.MESH
 LANES = 128
+PLANE = 16
 CHUNK = 16
 GROUP = 8
 MIB = 1024 * 1024
@@ -30,15 +31,19 @@
 def remap_kernel(
     flux,
     state,
+    area_atm_in,
+    area_ocean_in,
+    tiles,
+    tile_row_in,
+    tile_col_in,
+    tile_count,
+    ocean_own,
+    back_core,
+    ratios,
     area_atm,
     area_ocean,
-    tiles,
     tile_row,
     tile_col,
-    tile_count,
-    ocean_out,
-    atm_out,
-    sums_out,
     flux_own,
     flux_low,
     flux_high,
@@ -49,24 +54,25 @@
     flux_split,
     back_chain,
     ocean_chain,
-    back_core,
     send_low,
     send_high,
     got_low,
     got_high,
     ones_back,
-    ocean_own,
+    ones_low,
+    ones_high,
     table,
     index,
     mine,
     landed,
-    total,
+    entered,
     load_sem,
     tile_sem,
     index_sem,
-    store_sem,
     flux_send_sem,
     flux_recv_sem,
+    ones_send_sem,
+    ones_recv_sem,
     back_send_sem,
     back_recv_sem,
     sum_send_sem,
@@ -85,23 +91,49 @@
     window_span = atm_span + 2 * margin
     rim = margin * LANES
 
+    layers = count // PLANE
+    layer, place = me // PLANE, me % PLANE
+
     def partner(step):
         away = (step + 1) // 2
         shift = jnp.where(step % 2 == 0, away, -away)
         return (lax.rem(me + count // 2 + shift + count, count), core)
 
+    def plane_partner(step):
+        return (layer * PLANE + lax.rem(place + step, PLANE), core)
+
+    def line_partner(step):
+        return (lax.rem(layer + step, layers) * PLANE + place, core)
+
     barrier = pltpu.get_barrier_semaphore()
 
-    def greet(step, carry):
-        pl.semaphore_signal(barrier, inc=1, device_id=partner(step), device_id_type=MESH)
-        return carry
-
-    lax.fori_loop(0, count - 1, greet, 0)
-
-    load_state = pltpu.make_async_copy(state, state_own, load_sem.at[0])
-    load_flux = pltpu.make_async_copy(flux, flux_own, load_sem.at[1])
-    load_state.start()
-    load_flux.start()
+    def greet(semaphore, partner_of):
+        def one(step, carry):
+            pl.semaphore_signal(semaphore, inc=1, device_id=partner_of(step), device_id_type=MESH)
+            return carry
+
+        return one
+
+    for neighbour in (above, below):
+        pl.semaphore_signal(barrier, inc=1, device_id=neighbour, device_id_type=MESH)
+    lax.fori_loop(1, layers, greet(barrier, line_partner), 0)
+    lax.fori_loop(1, PLANE, greet(barrier, plane_partner), 0)
+
+    loads = [
+        pltpu.make_async_copy(source, target, load_sem.at[place])
+        for place, (source, target) in enumerate(
+            (
+                (tile_row_in, tile_row),
+                (tile_col_in, tile_col),
+                (area_ocean_in, area_ocean),
+                (state, state_own),
+                (area_atm_in, area_atm),
+                (flux, flux_own),
+            )
+        )
+    ]
+    for load in loads:
+        load.start()
     chunks = slots // CHUNK
 
     def load_tiles(chunk):
@@ -111,6 +143,8 @@
     for chunk in range(chunks):
         load_tiles(chunk).start()
 
+    for load in loads[0:2]:
+        load.wait()
     slot_of_row = lax.broadcasted_iota(jnp.int32, (slots, LANES), 0)
     lane = lax.broadcasted_iota(jnp.int32, (slots, LANES), 1)
     live = slot_of_row < tile_count[0]
@@ -131,15 +165,16 @@
     col_names = jnp.clip(col_names, 0, window_span - 1)
     row_former, row_last = chain_of(row_names)
     col_former, col_last = chain_of(col_names)
-    for place, row in enumerate(
+    for line, row in enumerate(
         (row_names, col_names, row_former, row_last, col_former, col_last)
     ):
-        table[place : place + 1, :] = row
+        table[line : line + 1, :] = row
     table[6:8, :] = jnp.zeros((2, LANES), jnp.int32)
     index_copy = pltpu.make_async_copy(table, index, index_sem)
     index_copy.start()
 
-    pl.semaphore_wait(barrier, count - 1)
+    pl.semaphore_wait(barrier, PLANE + layers)
+    lax.fori_loop(1, layers, greet(entered, line_partner), 0)
 
     def remote(source, target, sends, receives, place, device):
         return pltpu.make_async_remote_copy(
@@ -160,7 +195,8 @@
 
     zeros = jnp.zeros((fields, LANES), jnp.float32)
     extra = lax.broadcasted_iota(jnp.int32, (16, LANES), 0)
-    load_state.wait()
+    for load in loads[2:4]:
+        load.wait()
 
     def weigh(block, acc):
         area = area_ocean[:, lane_block(block)]
@@ -219,34 +255,58 @@
         return one
 
     got_atm = lax.fori_loop(0, margin, collect(send_low, 0), zeros)
+    got_atm = lax.fori_loop(0, margin, collect(send_high, margin + atm_span), got_atm)
+    ones_down = remote(
+        ones_back.at[pl.ds(0, margin)], ones_high, ones_send_sem, ones_recv_sem, 1, below
+    )
+    ones_up = remote(
+        ones_back.at[pl.ds(margin + atm_span, margin)],
+        ones_low,
+        ones_send_sem,
+        ones_recv_sem,
+        0,
+        above,
+    )
+    ones_down.start()
+    ones_up.start()
     back_down = remote(send_low, got_high, back_send_sem, back_recv_sem, 1, below)
+    back_up = remote(send_high, got_low, back_send_sem, back_recv_sem, 0, above)
     back_down.start()
-    got_atm = lax.fori_loop(0, margin, collect(send_high, margin + atm_span), got_atm)
-    back_up = remote(send_high, got_low, back_send_sem, back_recv_sem, 0, above)
     back_up.start()
     got_atm = lax.fori_loop(0, atm_span, collect(back_core, margin), got_atm)
 
-    load_flux.wait()
-
-    def spread(source, first, own):
-        def one(block, acc):
-            values = source[:, lane_block(block)]
-            high, low = split(values)
+    for load in loads[4:6]:
+        load.wait()
+
+    def spread(source, first):
+        def one(block, carry):
+            high, low = split(source[:, lane_block(block)])
             flux_split[first + block, 0:fields, :] = high
             flux_split[first + block, fields : 2 * fields, :] = low
-            got = acc[1] + values * ones_back[first + block]
-            if own:
-                return acc[0] + values * area_atm[:, lane_block(block)], got
-            return acc[0], got
+            return carry
 
         return one
 
-    acc = lax.fori_loop(0, atm_span, spread(flux_own, margin, True), (zeros, zeros))
-    flux_up.wait_recv()
-    flux_down.wait_recv()
-    acc = lax.fori_loop(0, margin, spread(flux_low, 0, False), acc)
-    target_ocean, got_ocean = lax.fori_loop(
-        0, margin, spread(flux_high, margin + atm_span, False), acc
+    def integrate(first, factors):
+        def one(block, acc):
+            return acc + flux_own[:, lane_block(first + block)] * factors(block)
+
+        return one
+
+    lax.fori_loop(0, atm_span, spread(flux_own, margin), 0)
+    target_ocean = lax.fori_loop(
+        0, atm_span, integrate(0, lambda block: area_atm[:, lane_block(block)]), zeros
+    )
+    ones_up.wait_recv()
+    ones_down.wait_recv()
+    got_ocean = lax.fori_loop(
+        0, margin, integrate(0, lambda block: ones_back[margin + block] + ones_low[block]), zeros
+    )
+    got_ocean = lax.fori_loop(
+        0,
+        margin,
+        integrate(margin, lambda block: ones_back[2 * margin + block] + ones_high[block]),
+        got_ocean,
     )
 
     stacked = jnp.concatenate([target_ocean, got_ocean, target_atm, got_atm], axis=0)
@@ -263,7 +323,13 @@
         ).start()
         return carry
 
+    pl.semaphore_wait(entered, layers - 1)
     lax.fori_loop(0, count - 1, send_row, 0)
+
+    flux_up.wait_recv()
+    flux_down.wait_recv()
+    lax.fori_loop(0, margin, spread(flux_low, 0), 0)
+    lax.fori_loop(0, margin, spread(flux_high, margin + atm_span), 0)
 
     def forward(step, carry):
         for part in range(GROUP):
@@ -286,37 +352,40 @@
         return carry
 
     lax.fori_loop(0, ocean_span, place_ocean, 0)
-    store_ocean = pltpu.make_async_copy(ocean_own, ocean_out, store_sem.at[0])
-    store_ocean.start()
 
     back_up.wait_recv()
     back_down.wait_recv()
     half = atm_cells - rim
     back_core[:, 0:rim] = (back_core[:, 0:rim] + got_low[...]) / area_atm[:, 0:rim]
     back_core[:, half:] = (back_core[:, half:] + got_high[...]) / area_atm[:, half:]
-    store_atm = pltpu.make_async_copy(back_core, atm_out, store_sem.at[1])
-    store_atm.start()
 
     pltpu.make_async_copy(landed, landed, sum_recv_sem).wait()
-    total[...] = mine[...] + jnp.sum(landed[...], axis=0)
-    store_sums = pltpu.make_async_copy(total, sums_out, store_sem.at[2])
-    store_sums.start()
-    for copy in (flux_up, flux_down, back_up, back_down):
+    sums = mine[...] + jnp.sum(landed[...], axis=0)
+    columns = jnp.transpose(jnp.broadcast_to(sums, (LANES, LANES)))
+    ratios[0] = columns[0:fields] / columns[fields : 2 * fields]
+    ratios[1] = columns[2 * fields : 3 * fields] / columns[3 * fields :]
+    for copy in (flux_up, flux_down, ones_up, ones_down, back_up, back_down):
         copy.wait_send()
     pltpu.make_async_copy(landed, landed, sum_send_sem).wait()
-    store_ocean.wait()
-    store_atm.wait()
-    store_sums.wait()
-
-
-def scale_kernel(ocean, atm, sums, ocean_out, atm_out):
-    fields = ocean.shape[0]
-    columns = jnp.transpose(jnp.broadcast_to(sums[...], (LANES, LANES)))
-    target_ocean, got_ocean, target_atm, got_atm = (
-        columns[part * fields : (part + 1) * fields, 0:1] for part in range(4)
-    )
-    ocean_out[...] = ocean[...] * (target_ocean / got_ocean)
-    atm_out[...] = atm[...] * (target_atm / got_atm)
+
+
+def scale_kernel(ocean, atm, ratios, ocean_out, atm_out, ocean_own, atm_own, store_sem):
+    stores = []
+    for part in range(ocean.shape[0] // 8):
+        rows = pl.ds(part * 8, 8)
+        for place, (source, own, target) in enumerate(
+            ((ocean, ocean_own, ocean_out), (atm, atm_own, atm_out))
+        ):
+            ratio = ratios[place, rows, :]
+            for block in range(source.shape[1] // LANES):
+                cells = pl.ds(block * LANES, LANES)
+                own[rows, cells] = source[rows, cells] * ratio
+            stores.append(
+                pltpu.make_async_copy(own.at[rows], target.at[rows], store_sem.at[part, place])
+            )
+            stores[-1].start()
+    for store in stores:
+        store.wait()
 
 
 def on_device(atm_flux, ocean_state, area_atm, area_ocean, tiles, tile_row, tile_col, tile_count):
@@ -329,19 +398,22 @@
     window_span = atm_span + 2 * margin
     rim = margin * LANES
     f32, bf16 = jnp.float32, jnp.bfloat16
-    anywhere = pl.BlockSpec(memory_space=pl.ANY)
+    hbm = pl.BlockSpec(memory_space=pltpu.HBM)
     vmem = pl.BlockSpec(memory_space=pltpu.VMEM)
-    smem = pl.BlockSpec(memory_space=pltpu.SMEM)
-    ocean_raw, atm_raw, sums = pl.pallas_call(
+    ocean_raw, atm_raw, ratios = pl.pallas_call(
         remap_kernel,
         out_shape=(
-            jax.ShapeDtypeStruct((fields, ocean_cells), f32),
-            jax.ShapeDtypeStruct((fields, atm_cells), f32),
-            jax.ShapeDtypeStruct((1, LANES), f32),
+            pltpu.VMEM((fields, ocean_cells), f32),
+            pltpu.VMEM((fields, atm_cells), f32),
+            pltpu.VMEM((2, fields, LANES), f32),
         ),
-        in_specs=[anywhere, anywhere, vmem, vmem, anywhere, vmem, vmem, smem],
-        out_specs=(anywhere, anywhere, anywhere),
+        in_specs=[hbm] * 7 + [pl.BlockSpec(memory_space=pltpu.SMEM)],
+        out_specs=(vmem, vmem, vmem),
         scratch_shapes=[
+            pltpu.VMEM((1, atm_cells), f32),
+            pltpu.VMEM((1, ocean_cells), f32),
+            pltpu.VMEM((1, slots), jnp.int32),
+            pltpu.VMEM((1, slots), jnp.int32),
             pltpu.VMEM((fields, atm_cells), f32),
             pltpu.VMEM((fields, rim), f32),
             pltpu.VMEM((fields, rim), f32),
@@ -352,22 +424,23 @@
             pltpu.VMEM((window_span, 2 * fields, LANES), bf16),
             pltpu.VMEM((slots + 1, fields + 8, LANES), f32),
             pltpu.VMEM((slots + 1, fields, LANES), f32),
-            pltpu.VMEM((fields, atm_cells), f32),
             pltpu.VMEM((fields, rim), f32),
             pltpu.VMEM((fields, rim), f32),
             pltpu.VMEM((fields, rim), f32),
             pltpu.VMEM((fields, rim), f32),
             pltpu.VMEM((window_span, 1, LANES), f32),
-            pltpu.VMEM((fields, ocean_cells), f32),
+            pltpu.VMEM((margin, 1, LANES), f32),
+            pltpu.VMEM((margin, 1, LANES), f32),
             pltpu.VMEM((8, LANES), jnp.int32),
             pltpu.SMEM((8, LANES), jnp.int32),
             pltpu.VMEM((1, LANES), f32),
             pltpu.VMEM((devices - 1, 1, LANES), f32),
-            pltpu.VMEM((1, LANES), f32),
-            pltpu.SemaphoreType.DMA((2,)),
+            pltpu.SemaphoreType.REGULAR,
+            pltpu.SemaphoreType.DMA((6,)),
             pltpu.SemaphoreType.DMA((slots // CHUNK,)),
             pltpu.SemaphoreType.DMA,
-            pltpu.SemaphoreType.DMA((3,)),
+            pltpu.SemaphoreType.DMA((2,)),
+            pltpu.SemaphoreType.DMA((2,)),
             pltpu.SemaphoreType.DMA((2,)),
             pltpu.SemaphoreType.DMA((2,)),
             pltpu.SemaphoreType.DMA((2,)),
@@ -376,37 +449,40 @@
             pltpu.SemaphoreType.DMA,
         ],
         compiler_params=pltpu.CompilerParams(
-            collective_id=0, has_side_effects=True, vmem_limit_bytes=48 * MIB
+            collective_id=0, has_side_effects=True, vmem_limit_bytes=40 * MIB
         ),
         name="remap",
     )(
-        atm_flux,
-        ocean_state,
-        area_atm.reshape(1, atm_cells),
-        area_ocean.reshape(1, ocean_cells),
-        tiles,
-        tile_row.reshape(1, slots),
-        tile_col.reshape(1, slots),
+        *(
+            pltpu.with_memory_space_constraint(operand, pltpu.HBM)
+            for operand in (
+                atm_flux,
+                ocean_state,
+                area_atm.reshape(1, atm_cells),
+                area_ocean.reshape(1, ocean_cells),
+                tiles,
+                tile_row.reshape(1, slots),
+                tile_col.reshape(1, slots),
+            )
+        ),
         tile_count,
     )
     return pl.pallas_call(
         scale_kernel,
-        grid=(4,),
         out_shape=(
             jax.ShapeDtypeStruct((fields, ocean_cells), f32),
             jax.ShapeDtypeStruct((fields, atm_cells), f32),
         ),
-        in_specs=[
-            pl.BlockSpec((fields, ocean_cells // 4), lambda step: (0, step)),
-            pl.BlockSpec((fields, atm_cells // 4), lambda step: (0, step)),
-            pl.BlockSpec((1, LANES), lambda step: (0, 0)),
+        in_specs=[vmem] * 3,
+        out_specs=(hbm, hbm),
+        scratch_shapes=[
+            pltpu.VMEM((fields, ocean_cells), f32),
+            pltpu.VMEM((fields, atm_cells), f32),
+            pltpu.SemaphoreType.DMA((fields // 8, 2)),
         ],
-        out_specs=(
-            pl.BlockSpec((fields, ocean_cells // 4), lambda step: (0, step)),
-            pl.BlockSpec((fields, atm_cells // 4), lambda step: (0, step)),
-        ),
+        compiler_params=pltpu.CompilerParams(vmem_limit_bytes=8 * MIB),
         name="scale",
-    )(ocean_raw, atm_raw, sums)
+    )(ocean_raw, atm_raw, ratios)
 
 
 def solution(mesh):

time: 45 us -> 32.8 us (0.73)
  the two profiles are of different devices: /device:TPU:8 before, /device:TPU:1 now
where the time goes in v3:
time: 32.8 us; the launch traced here: 32.7 us
  Pallas kernels  31.4 us (96%)
  between operations  1.29 us (4%)
    pallas_call x1, Pallas kernels, on_device(): pl.pallas_call(remap_kernel, out_shape=(pltpu.VMEM((fields, ocean_cells),...  30.2 us
    pallas_call x1, Pallas kernels, on_device(): pl.pallas_call(scale_kernel, out_shape=(jax.ShapeDtypeStruct((fields, oce...  1.22 us

profile of v3, /device:TPU:1, one launch (start us, length us, event | category | flops | bytes accessed | tf_op | source)
XLA Modules:
  0.0 32.7 jit_solution(8342750707656195809)
XLA Ops:
  1.3 30.2 %remap.1 = (f32[32,8192]{1,0:T(8,128)S(1)}, f32[32,4096]{1,0:T(8,128)S(1)}, f32[2,32,128]{2,1,0:T(8,128)S(1)}) custom-call(f32[32,4096]{1,0:T(8,128)} %flux.1, f32[32,8192]{1,0:T(8,128)} %state.1, f32[1,4096]{1,0:T(1,128)} %bitcast.5, f32[1,8192]{1,0:T(1,128)} %bitcast.4, f32[128,128,128]{2,1,0:T(8,128)} %tiles.1, s32[1,128]{1,0:T(1,128)} %bitcast.6, ...), custom_call_target="tpu_custom_call" | custom-call | tf_op jit(solution)/shard_map/remap/pallas_call | solution.py:403
  31.5 1.2 %scale.1 = (f32[32,8192]{1,0:T(8,128)}, f32[32,4096]{1,0:T(8,128)}) custom-call(f32[32,8192]{1,0:T(8,128)S(1)} %get-tuple-element.5.ocean, f32[32,4096]{1,0:T(8,128)S(1)} %get-tuple-element.6.atm, f32[2,32,128]{2,1,0:T(8,128)S(1)} %get-tuple-element.7.ratios), custom_call_target="tpu_custom_call" | custom-call | tf_op jit(solution)/shard_map/scale/pallas_call | solution.py:470

commit v4 on v3

--- a/solution.py
+++ b/solution.py
@@ -10,8 +10,7 @@
 MESH = pl.DeviceIdType.MESH
 LANES = 128
 PLANE = 16
-CHUNK = 16
-GROUP = 8
+CHUNK = 32
 MIB = 1024 * 1024
 
 
@@ -49,7 +48,7 @@
     flux_high,
     state_own,
     tiles_own,
-    tiles_split,
+    tiles_turned,
     state_split,
     flux_split,
     back_chain,
@@ -132,7 +131,7 @@
             )
         )
     ]
-    for load in loads:
+    for load in loads[0:4]:
         load.start()
     chunks = slots // CHUNK
 
@@ -142,6 +141,8 @@
 
     for chunk in range(chunks):
         load_tiles(chunk).start()
+    for load in loads[4:6]:
+        load.start()
 
     for load in loads[0:2]:
         load.wait()
@@ -173,9 +174,6 @@
     index_copy = pltpu.make_async_copy(table, index, index_sem)
     index_copy.start()
 
-    pl.semaphore_wait(barrier, PLANE + layers)
-    lax.fori_loop(1, layers, greet(entered, line_partner), 0)
-
     def remote(source, target, sends, receives, place, device):
         return pltpu.make_async_remote_copy(
             src_ref=source,
@@ -186,12 +184,35 @@
             device_id_type=MESH,
         )
 
-    flux_up = remote(
-        flux.at[:, pl.ds(atm_cells - rim, rim)], flux_low, flux_send_sem, flux_recv_sem, 0, above
-    )
-    flux_down = remote(flux.at[:, pl.ds(0, rim)], flux_high, flux_send_sem, flux_recv_sem, 1, below)
-    flux_up.start()
-    flux_down.start()
+    pl.semaphore_wait(barrier, PLANE + layers)
+    lax.fori_loop(1, layers, greet(entered, line_partner), 0)
+
+    half_fields = fields // 2
+    flux_sends = []
+    for half in range(2):
+        rows = pl.ds(half * half_fields, half_fields)
+        flux_sends.append(
+            (
+                remote(
+                    flux.at[rows, pl.ds(atm_cells - rim, rim)],
+                    flux_low.at[rows],
+                    flux_send_sem,
+                    flux_recv_sem,
+                    2 * half,
+                    above,
+                ),
+                remote(
+                    flux.at[rows, pl.ds(0, rim)],
+                    flux_high.at[rows],
+                    flux_send_sem,
+                    flux_recv_sem,
+                    2 * half + 1,
+                    below,
+                ),
+            )
+        )
+    for copy in flux_sends[0]:
+        copy.start()
 
     zeros = jnp.zeros((fields, LANES), jnp.float32)
     extra = lax.broadcasted_iota(jnp.int32, (16, LANES), 0)
@@ -211,21 +232,23 @@
         state_split[block, 2 * fields : 2 * fields + 16, :] = area_rows.astype(jnp.bfloat16)
         return acc + weighted
 
-    target_atm = lax.fori_loop(0, ocean_span, weigh, zeros)
+    target_atm = lax.fori_loop(0, ocean_span, weigh, zeros, unroll=8)
 
     back_chain[0] = jnp.zeros(back_chain.shape[1:], jnp.float32)
     ocean_chain[0] = jnp.zeros(ocean_chain.shape[1:], jnp.float32)
     index_copy.wait()
 
-    def backward(step, carry):
-        for part in range(GROUP):
-            slot = step * GROUP + part
-            high, low = split(tiles_own[slot])
-            tiles_split[slot, 0] = high
-            tiles_split[slot, 1] = low
+    def backward(chunk, carry):
+        load_tiles(chunk).wait()
+        for part in range(CHUNK):
+            slot = chunk * CHUNK + part
+            weights = tiles_own[slot]
+            high, low = split(weights.T)
+            tiles_turned[slot, 0] = high
+            tiles_turned[slot, 1] = low
             terms = jnp.dot(
                 twice(state_split[index[0, slot]]),
-                jnp.concatenate([high, low], axis=0),
+                jnp.concatenate(split(weights), axis=0),
                 preferred_element_type=jnp.float32,
             )
             former = index[4, slot]
@@ -237,10 +260,7 @@
             )
         return carry
 
-    steps = CHUNK // GROUP
-    for chunk in range(chunks):
-        load_tiles(chunk).wait()
-        lax.fori_loop(chunk * steps, (chunk + 1) * steps, backward, 0)
+    lax.fori_loop(0, chunks, backward, 0)
 
     def collect(target, first):
         def one(block, acc):
@@ -254,8 +274,8 @@
 
         return one
 
-    got_atm = lax.fori_loop(0, margin, collect(send_low, 0), zeros)
-    got_atm = lax.fori_loop(0, margin, collect(send_high, margin + atm_span), got_atm)
+    got_atm = lax.fori_loop(0, margin, collect(send_low, 0), zeros, unroll=8)
+    got_atm = lax.fori_loop(0, margin, collect(send_high, margin + atm_span), got_atm, unroll=8)
     ones_down = remote(
         ones_back.at[pl.ds(0, margin)], ones_high, ones_send_sem, ones_recv_sem, 1, below
     )
@@ -269,11 +289,13 @@
     )
     ones_down.start()
     ones_up.start()
+    for copy in flux_sends[1]:
+        copy.start()
     back_down = remote(send_low, got_high, back_send_sem, back_recv_sem, 1, below)
     back_up = remote(send_high, got_low, back_send_sem, back_recv_sem, 0, above)
     back_down.start()
     back_up.start()
-    got_atm = lax.fori_loop(0, atm_span, collect(back_core, margin), got_atm)
+    got_atm = lax.fori_loop(0, atm_span, collect(back_core, margin), got_atm, unroll=8)
 
     for load in loads[4:6]:
         load.wait()
@@ -293,20 +315,25 @@
 
         return one
 
-    lax.fori_loop(0, atm_span, spread(flux_own, margin), 0)
+    lax.fori_loop(0, atm_span, spread(flux_own, margin), 0, unroll=8)
     target_ocean = lax.fori_loop(
-        0, atm_span, integrate(0, lambda block: area_atm[:, lane_block(block)]), zeros
+        0, atm_span, integrate(0, lambda block: area_atm[:, lane_block(block)]), zeros, unroll=8
     )
     ones_up.wait_recv()
     ones_down.wait_recv()
     got_ocean = lax.fori_loop(
-        0, margin, integrate(0, lambda block: ones_back[margin + block] + ones_low[block]), zeros
+        0,
+        margin,
+        integrate(0, lambda block: ones_back[margin + block] + ones_low[block]),
+        zeros,
+        unroll=8,
     )
     got_ocean = lax.fori_loop(
         0,
         margin,
         integrate(margin, lambda block: ones_back[2 * margin + block] + ones_high[block]),
         got_ocean,
+        unroll=8,
     )
 
     stacked = jnp.concatenate([target_ocean, got_ocean, target_atm, got_atm], axis=0)
@@ -326,18 +353,17 @@
     pl.semaphore_wait(entered, layers - 1)
     lax.fori_loop(0, count - 1, send_row, 0)
 
-    flux_up.wait_recv()
-    flux_down.wait_recv()
-    lax.fori_loop(0, margin, spread(flux_low, 0), 0)
-    lax.fori_loop(0, margin, spread(flux_high, margin + atm_span), 0)
-
-    def forward(step, carry):
-        for part in range(GROUP):
-            slot = step * GROUP + part
-            terms = lax.dot_general(
+    for copy in flux_sends[0] + flux_sends[1]:
+        copy.wait_recv()
+    lax.fori_loop(0, margin, spread(flux_low, 0), 0, unroll=8)
+    lax.fori_loop(0, margin, spread(flux_high, margin + atm_span), 0, unroll=8)
+
+    def forward(chunk, carry):
+        for part in range(CHUNK):
+            slot = chunk * CHUNK + part
+            terms = jnp.dot(
                 twice(flux_split[index[1, slot]]),
-                jnp.concatenate([tiles_split[slot, 0], tiles_split[slot, 1]], axis=1),
-                (((1,), (1,)), ((), ())),
+                jnp.concatenate([tiles_turned[slot, 0], tiles_turned[slot, 1]], axis=0),
                 preferred_element_type=jnp.float32,
             )
             ocean_chain[slot + 1] = (
@@ -345,13 +371,13 @@
             )
         return carry
 
-    lax.fori_loop(0, slots // GROUP, forward, 0)
+    lax.fori_loop(0, chunks, forward, 0)
 
     def place_ocean(block, carry):
         ocean_own[:, lane_block(block)] = ocean_chain[index[3, block]]
         return carry
 
-    lax.fori_loop(0, ocean_span, place_ocean, 0)
+    lax.fori_loop(0, ocean_span, place_ocean, 0, unroll=8)
 
     back_up.wait_recv()
     back_down.wait_recv()
@@ -364,7 +390,7 @@
     columns = jnp.transpose(jnp.broadcast_to(sums, (LANES, LANES)))
     ratios[0] = columns[0:fields] / columns[fields : 2 * fields]
     ratios[1] = columns[2 * fields : 3 * fields] / columns[3 * fields :]
-    for copy in (flux_up, flux_down, ones_up, ones_down, back_up, back_down):
+    for copy in (*flux_sends[0], *flux_sends[1], ones_up, ones_down, back_up, back_down):
         copy.wait_send()
     pltpu.make_async_copy(landed, landed, sum_send_sem).wait()
 
@@ -439,8 +465,8 @@
             pltpu.SemaphoreType.DMA((6,)),
             pltpu.SemaphoreType.DMA((slots // CHUNK,)),
             pltpu.SemaphoreType.DMA,
-            pltpu.SemaphoreType.DMA((2,)),
-            pltpu.SemaphoreType.DMA((2,)),
+            pltpu.SemaphoreType.DMA((4,)),
+            pltpu.SemaphoreType.DMA((4,)),
             pltpu.SemaphoreType.DMA((2,)),
             pltpu.SemaphoreType.DMA((2,)),
             pltpu.SemaphoreType.DMA((2,)),

time: 32.8 us -> 30.7 us (0.936)
  the two profiles are of different devices: /device:TPU:1 before, /device:TPU:8 now
where the time goes in v4:
time: 30.7 us; the launch traced here: 30.2 us
  Pallas kernels  28.9 us (94%)
  between operations  1.29 us (4%)
    pallas_call x1, Pallas kernels, on_device(): pl.pallas_call(remap_kernel, out_shape=(pltpu.VMEM((fields, ocean_cells),...  27.7 us
    pallas_call x1, Pallas kernels, on_device(): pl.pallas_call(scale_kernel, out_shape=(jax.ShapeDtypeStruct((fields, oce...  1.22 us

profile of v4, /device:TPU:8, one launch (start us, length us, event | category | flops | bytes accessed | tf_op | source)
XLA Modules:
  0.0 30.2 jit_solution(15900553413802964844)
XLA Ops:
  1.3 27.7 %remap.1 = (f32[32,8192]{1,0:T(8,128)S(1)}, f32[32,4096]{1,0:T(8,128)S(1)}, f32[2,32,128]{2,1,0:T(8,128)S(1)}) custom-call(f32[32,4096]{1,0:T(8,128)} %flux.1, f32[32,8192]{1,0:T(8,128)} %state.1, f32[1,4096]{1,0:T(1,128)} %bitcast.5, f32[1,8192]{1,0:T(1,128)} %bitcast.4, f32[128,128,128]{2,1,0:T(8,128)} %tiles.1, s32[1,128]{1,0:T(1,128)} %bitcast.6, ...), custom_call_target="tpu_custom_call" | custom-call | tf_op jit(solution)/shard_map/remap/pallas_call | solution.py:429
  29.0 1.2 %scale.1 = (f32[32,8192]{1,0:T(8,128)}, f32[32,4096]{1,0:T(8,128)}) custom-call(f32[32,8192]{1,0:T(8,128)S(1)} %get-tuple-element.5.ocean, f32[32,4096]{1,0:T(8,128)S(1)} %get-tuple-element.6.atm, f32[2,32,128]{2,1,0:T(8,128)S(1)} %get-tuple-element.7.ratios), custom_call_target="tpu_custom_call" | custom-call | tf_op jit(solution)/shard_map/scale/pallas_call | solution.py:496

commit v5 on v4

--- a/solution.py
+++ b/solution.py
@@ -93,30 +93,25 @@
     layers = count // PLANE
     layer, place = me // PLANE, me % PLANE
 
-    def partner(step):
-        away = (step + 1) // 2
-        shift = jnp.where(step % 2 == 0, away, -away)
-        return (lax.rem(me + count // 2 + shift + count, count), core)
+    def partner(away):
+        return (lax.bitwise_and(me + away, count - 1), core)
 
     def plane_partner(step):
-        return (layer * PLANE + lax.rem(place + step, PLANE), core)
+        return (layer * PLANE + lax.bitwise_and(place + step, PLANE - 1), core)
 
     def line_partner(step):
-        return (lax.rem(layer + step, layers) * PLANE + place, core)
+        return (lax.bitwise_and(layer + step, layers - 1) * PLANE + place, core)
 
     barrier = pltpu.get_barrier_semaphore()
 
-    def greet(semaphore, partner_of):
-        def one(step, carry):
+    def greet(semaphore, partner_of, partners):
+        for step in range(1, partners):
             pl.semaphore_signal(semaphore, inc=1, device_id=partner_of(step), device_id_type=MESH)
-            return carry
-
-        return one
 
     for neighbour in (above, below):
         pl.semaphore_signal(barrier, inc=1, device_id=neighbour, device_id_type=MESH)
-    lax.fori_loop(1, layers, greet(barrier, line_partner), 0)
-    lax.fori_loop(1, PLANE, greet(barrier, plane_partner), 0)
+    greet(barrier, line_partner, layers)
+    greet(barrier, plane_partner, PLANE)
 
     loads = [
         pltpu.make_async_copy(source, target, load_sem.at[place])
@@ -185,7 +180,7 @@
         )
 
     pl.semaphore_wait(barrier, PLANE + layers)
-    lax.fori_loop(1, layers, greet(entered, line_partner), 0)
+    greet(entered, line_partner, layers)
 
     half_fields = fields // 2
     flux_sends = []
@@ -275,10 +270,11 @@
         return one
 
     got_atm = lax.fori_loop(0, margin, collect(send_low, 0), zeros, unroll=8)
-    got_atm = lax.fori_loop(0, margin, collect(send_high, margin + atm_span), got_atm, unroll=8)
     ones_down = remote(
         ones_back.at[pl.ds(0, margin)], ones_high, ones_send_sem, ones_recv_sem, 1, below
     )
+    ones_down.start()
+    got_atm = lax.fori_loop(0, margin, collect(send_high, margin + atm_span), got_atm, unroll=8)
     ones_up = remote(
         ones_back.at[pl.ds(margin + atm_span, margin)],
         ones_low,
@@ -287,7 +283,6 @@
         0,
         above,
     )
-    ones_down.start()
     ones_up.start()
     for copy in flux_sends[1]:
         copy.start()
@@ -339,19 +334,24 @@
     stacked = jnp.concatenate([target_ocean, got_ocean, target_atm, got_atm], axis=0)
     mine[...] = jnp.sum(jnp.transpose(stacked), axis=0, keepdims=True)
 
-    def send_row(step, carry):
+    def send_row(away, slot):
         pltpu.make_async_remote_copy(
             src_ref=mine,
-            dst_ref=landed.at[step],
+            dst_ref=landed.at[slot],
             send_sem=sum_send_sem,
             recv_sem=sum_recv_sem,
-            device_id=partner(step),
+            device_id=partner(away),
             device_id_type=MESH,
         ).start()
+
+    def send_pair(step, carry):
+        send_row(count // 2 + step, 2 * step)
+        send_row(count // 2 - step, 2 * step - 1)
         return carry
 
     pl.semaphore_wait(entered, layers - 1)
-    lax.fori_loop(0, count - 1, send_row, 0)
+    send_row(count // 2, 0)
+    lax.fori_loop(1, count // 2, send_pair, 0, unroll=3)
 
     for copy in flux_sends[0] + flux_sends[1]:
         copy.wait_recv()

time: 30.7 us -> 30.6 us (level)
  no operation moved by 1% of the time
where the time goes in v5:
time: 30.6 us; the launch traced here: 30.1 us
  Pallas kernels  28.9 us (94%)
  between operations  1.29 us (4%)
    pallas_call x1, Pallas kernels, on_device(): pl.pallas_call(remap_kernel, out_shape=(pltpu.VMEM((fields, ocean_cells),...  27.6 us
    pallas_call x1, Pallas kernels, on_device(): pl.pallas_call(scale_kernel, out_shape=(jax.ShapeDtypeStruct((fields, oce...  1.22 us

profile of v5, /device:TPU:8, one launch (start us, length us, event | category | flops | bytes accessed | tf_op | source)
XLA Modules:
  0.0 30.1 jit_solution(3939895417197487354)
XLA Ops:
  1.3 27.6 %remap.1 = (f32[32,8192]{1,0:T(8,128)S(1)}, f32[32,4096]{1,0:T(8,128)S(1)}, f32[2,32,128]{2,1,0:T(8,128)S(1)}) custom-call(f32[32,4096]{1,0:T(8,128)} %flux.1, f32[32,8192]{1,0:T(8,128)} %state.1, f32[1,4096]{1,0:T(1,128)} %bitcast.5, f32[1,8192]{1,0:T(1,128)} %bitcast.4, f32[128,128,128]{2,1,0:T(8,128)} %tiles.1, s32[1,128]{1,0:T(1,128)} %bitcast.6, ...), custom_call_target="tpu_custom_call" | custom-call | tf_op jit(solution)/shard_map/remap/pallas_call | solution.py:429
  28.9 1.2 %scale.1 = (f32[32,8192]{1,0:T(8,128)}, f32[32,4096]{1,0:T(8,128)}) custom-call(f32[32,8192]{1,0:T(8,128)S(1)} %get-tuple-element.5.ocean, f32[32,4096]{1,0:T(8,128)S(1)} %get-tuple-element.6.atm, f32[2,32,128]{2,1,0:T(8,128)S(1)} %get-tuple-element.7.ratios), custom_call_target="tpu_custom_call" | custom-call | tf_op jit(solution)/shard_map/scale/pallas_call | solution.py:496
